TPU v7x, 32 devices: a whole 2x2x4 slice. The times are simulated.
32 devices in a mesh: groups: 2 (over x), sample: 8 (over z, y), feature: 2 (over core).
Axes of the slice: x: 2, y: 2, z: 4, core: 2. Of those that a mesh axis runs over, the one named last changes fastest.
Arguments:
- blk_values: bfloat16 [16, 2, 320, 128, 128], P(('groups', 'sample'), 'feature'), parts along dimension 0, may hold values from -6 to 6
- blk_rows: int32 [16, 2, 320], P(('groups', 'sample'), 'feature'), parts along dimension 0, may hold values from 0 to 31
- blk_cols: int32 [16, 2, 320], P(('groups', 'sample'), 'feature'), parts along dimension 0, may hold values from 0 to 1023, as said below
- blk_count: int32 [16, 2], P(('groups', 'sample'), 'feature'), parts along dimension 0, may hold values from 1 to 320, as said below
- boot_counts: int32 [65536, 32], P(('groups', 'sample')), parts along dimension 0, may hold values from 0 to 8, as said below
- labels: int32 [65536], P(('groups', 'sample')), parts along dimension 0, may hold values 0 or 1
- coefs: float32 [524288, 32], P(('groups', 'feature', 'sample')), parts along dimension 0, may hold values from -0.18 to 0.18
Outputs:
- gradient: float32 [524288, 32], P(('groups', 'feature', 'sample')), parts along dimension 0
There are 2 independent parts, one for each index of `groups`. A program takes and returns all parts, laid end to end along the dimension named above; each array names one. Nothing has to cross between parts.
Inputs may be any that keep to these rules, and one draw needn't show every extreme that they name: `blk_cols`: of all 320 slots of one device, at most 40 name column blocks within one index of sample's share of the columns (the share of index k is blocks k * 262144 / (2 * 8 * 128) onward); every device reaches 40. `blk_count`: slots at or beyond a device's count hold no part of the design; some device has all 320 slots live. `boot_counts`: some entry reaches the most.
All inputs are finite; a program needn't handle non-finite values. No bound on the sum of `labels` on one device may be relied on, other than what follows from the above.
Results may differ from a plain program's by a relative error of at most 0.0031.
Values may be sent and summed in bfloat16 or wider, within the bound.
A program may use at most 128 MiB of HBM per device.

v0:
```python
import jax
import jax.numpy as jnp
from jax import lax
from jax.sharding import PartitionSpec as P


def local(blk_values, blk_rows, blk_cols, blk_count, boot_counts, labels, coefs):
    values = blk_values[0, 0]
    rows = blk_rows[0, 0]
    cols = blk_cols[0, 0]
    count = blk_count[0, 0]
    slots = values.shape[0]
    width = values.shape[1]
    reps = coefs.shape[1]
    owners_total = lax.axis_size("sample")
    row_blocks = boot_counts.shape[0] // width
    col_blocks = coefs.shape[0] * owners_total // width
    live = (jnp.arange(slots, dtype=jnp.int32) < count).astype(jnp.float32)[:, None, None]
    coef_low = coefs.astype(jnp.bfloat16)
    whole = lax.all_gather(coef_low, "sample", axis=0, tiled=True).reshape(col_blocks, width, reps)
    products = jnp.einsum("bij,bjr->bir", values, whole[cols], preferred_element_type=jnp.float32)
    products = products * live
    partial_value = jax.ops.segment_sum(products, rows, num_segments=row_blocks).reshape(
        row_blocks * width, reps
    )
    counts_all = boot_counts.astype(jnp.float32)
    labels_all = labels.astype(jnp.float32)[:, None]
    margins = lax.psum(partial_value, "feature")
    resid = (counts_all * (jax.nn.sigmoid(margins) - labels_all)).astype(jnp.bfloat16)
    picked_rows = resid.reshape(row_blocks, width, reps)[rows]
    back = (
        jnp.einsum("bij,bir->bjr", values, picked_rows, preferred_element_type=jnp.float32) * live
    )
    term = jax.ops.segment_sum(back, cols, num_segments=col_blocks).reshape(
        col_blocks * width, reps
    )
    return lax.psum_scatter(term, "sample", scatter_dimension=0, tiled=True) / 16.0


def solution(mesh):
    return jax.shard_map(
        local,
        mesh=mesh,
        in_specs=(
            P(("groups", "sample"), "feature", None, None, None),
            P(("groups", "sample"), "feature", None),
            P(("groups", "sample"), "feature", None),
            P(("groups", "sample"), "feature"),
            P(("groups", "sample"), None),
            P(("groups", "sample")),
            P(("groups", "feature", "sample"), None),
        ),
        out_specs=P(("groups", "feature", "sample"), None),
        check_vma=False,
    )
```

profile of v0, /device:TPU:14, one launch (start us, length us, event | category | flops | bytes accessed | tf_op | source)
XLA Modules:
  0.0 569.6 jit_solution(12885315595506288512)
XLA Ops:
  6.5 2.7 convert_element_type.20
  9.2 0.0 all-gather.2.cloned.1.call-update
  9.2 0.0 all-reduce.2.cloned.1.call-start
  9.9 0.7 reduce.1
  10.6 0.7 fusion.10
  11.3 121.5 %all-gather.2.cloned.1.call-done = bf16[131072,32]{0,1:T(8,128)(2,1)} async-done(((bf16[16384,32]{0,1:T(8,128)(2,1)}), bf16[131072,32]{0,1:T(8,128)(2,1)}) %all-gather.2.cloned.1.call-update) | async-done | bytes 8388624 | tf_op jit(solution)/shard_map/all_gather | solution.py:20
  132.8 8.0 %copy_bitcast_fusion.1 = bf16[1024,128,32]{1,2,0:T(8,128)(2,1)} fusion(bf16[131072,32]{0,1:T(8,128)(2,1)} %all-gather.2.cloned.1.call-done), kind=kLoop, calls=%fused_computation.9 | loop fusion | bytes 16777216 | tf_op jit(solution)/shard_map/reshape | solution.py:20
  140.8 4.5 gather_fusion
  145.4 9.7 %multiply_bitcast_fusion.1 = f32[320,128,32]{1,2,0:T(8,128)} fusion(f32[320]{0:T(512)S(1)} %fusion.9, bf16[320,128,32]{1,2,0:T(8,128)(2,1)S(1)} %gather_fusion, bf16[1,1,320,128,128]{4,3,2,1,0:T(8,128)(2,1)} %param.7), kind=kOutput, calls=%fused_computation.11 | convolution fusion | flops 336855040 | bytes 18351360 | tf_op jit(solution)/shard_map/bij,bjr->bir/dot_general | solution.py:21
  155.2 0.0 copy-start.3
  155.2 28.8 %scatter_fusion = f32[32,128,32]{1,2,0:T(8,128)S(1)} fusion(f32[32,128,32]{1,2,0:T(8,128)S(1)} %broadcast_in_dim.5, s32[320]{0:T(512)S(1)} %reduce.1, f32[320,128,32]{1,2,0:T(8,128)} %multiply_bitcast_fusion.1), kind=kCustom, calls=%fused_computation.2 | custom fusion | flops 1310720 | bytes 15729920 | tf_op jit(solution)/shard_map/scatter-add | solution.py:23
  184.0 0.8 copy_bitcast_fusion.2
  184.9 0.0 all-reduce.2.cloned.1.call-update
  184.9 0.0 reduce-scatter.2.cloned.1.call-start
  185.0 20.0 %all-reduce.2.cloned.1.call-done = f32[4096,32]{0,1:T(8,128)} async-done(((f32[4096,32]{0,1:T(8,128)}), f32[4096,32]{0,1:T(8,128)}) %all-reduce.2.cloned.1.call-update) | async-done | bytes 524304 | tf_op jit(solution)/shard_map/psum | solution.py:28
  205.0 1.2 copy_bitcast_fusion.3
  206.2 2.3 gather_fusion.1
  208.5 7.1 %multiply_bitcast_fusion = f32[320,128,32]{1,2,0:T(8,128)} fusion(f32[320]{0:T(512)S(1)} %fusion.9, bf16[320,128,32]{1,2,0:T(8,128)(2,1)S(1)} %gather_fusion.1, bf16[1,1,320,128,128]{4,3,2,1,0:T(8,128)(2,1)} %param.7), kind=kOutput, calls=%fused_computation.10 | convolution fusion | flops 336855040 | bytes 18351360 | tf_op jit(solution)/shard_map/bij,bir->bjr/dot_general | solution.py:32
  215.6 7.9 %broadcast_in_dim.4 = f32[1024,128,32]{1,2,0:T(8,128)} broadcast(f32[]{:T(128)} %constant.6.clone.1), dimensions={} | broadcast | bytes 16777220 | tf_op jit(solution)/shard_map/broadcast_in_dim | solution.py:34
  223.5 42.8 %scatter_fusion.1 = f32[1024,128,32]{1,2,0:T(8,128)} fusion(f32[1024,128,32]{1,2,0:T(8,128)} %broadcast_in_dim.4, s32[320]{0:T(512)S(1)} %reduce, f32[320,128,32]{1,2,0:T(8,128)} %multiply_bitcast_fusion), kind=kCustom, calls=%fused_computation.3 | custom fusion | flops 1310720 | bytes 15729920 | tf_op jit(solution)/shard_map/scatter-add | solution.py:34
  266.3 11.3 %copy_bitcast_fusion = f32[131072,32]{0,1:T(8,128)} fusion(f32[1024,128,32]{1,2,0:T(8,128)} %scatter_fusion.1), kind=kLoop, calls=%fused_computation.4 | loop fusion | bytes 33554432 | tf_op jit(solution)/shard_map/reshape | solution.py:34
  277.6 0.0 reduce-scatter.2.cloned.1.call-update
  277.6 282.4 %reduce-scatter.2.cloned.1.call-done = f32[16384,32]{0,1:T(8,128)} async-done(((f32[131072,32]{0,1:T(8,128)}), f32[16384,32]{0,1:T(8,128)}) %reduce-scatter.2.cloned.1.call-update) | async-done | bytes 2097168 | tf_op jit(solution)/shard_map/reduce_scatter | solution.py:37
  560.0 3.0 broadcast_multiply_fusion
  (15 shorter events, 0.1 us)
Async XLA Ops:
  6.5 126.3 %all-gather.2.cloned.1.call-start = ((), (), s32[]{:S(2)}) async-start(), calls=%async_computation.1 | async-start | bytes 9437184 | tf_op jit(solution)/shard_map/all_gather | solution.py:20
  9.2 195.8 %all-reduce.2.cloned.1.call-start = ((), (), s32[]{:S(2)}) async-start(), calls=%async_computation.2 | async-start | bytes 1048576 | tf_op jit(solution)/shard_map/psum | solution.py:28
  155.1 29.8 %copy-start.2 = (s32[1,1,320]{2,1,0:T(1,128)S(1)}, s32[1,1,320]{2,1,0:T(1,128)}, u32[]{:S(2)}) copy-start(s32[1,1,320]{2,1,0:T(1,128)} %param.9) | copy-start | bytes 3844
  155.2 29.8 %copy-start.1 = (s32[4096]{0:T(1024)S(1)}, s32[4096]{0:T(1024)}, u32[]{:S(2)}) copy-start(s32[4096]{0:T(1024)} %param.12) | copy-start | bytes 49156
  155.2 29.8 %copy-start.3 = (s32[1,1,320]{2,1,0:T(1,128)S(1)}, s32[1,1,320]{2,1,0:T(1,128)}, u32[]{:S(2)}) copy-start(s32[1,1,320]{2,1,0:T(1,128)} %param.8) | copy-start | bytes 3844
  155.2 49.8 %copy-start = (s32[4096,32]{0,1:T(8,128)S(1)}, s32[4096,32]{0,1:T(8,128)}, u32[]{:S(2)}) copy-start(s32[4096,32]{0,1:T(8,128)} %param.11) | copy-start | bytes 1572868
  184.9 375.1 %reduce-scatter.2.cloned.1.call-start = ((), (), s32[]{:S(2)}) async-start(), calls=%async_computation.3 | async-start | bytes 18874368 | tf_op jit(solution)/shard_map/reduce_scatter | solution.py:37
Sparse Core Ops, SparseCore 0:
  9.5 123.2 all-gather.1
  185.0 19.9 all-reduce.1
  277.8 282.1 reduce-scatter.1
where the time goes:
time: 574 us; the launch traced here: 570 us
  waiting for transfers between devices  424 us (74%)
  other arithmetic  80 us (14%)
  local copies, waits for them, and re-layouts  35 us (6%)
  matrix products  16.8 us (3%)
  between operations  13.9 us (2%)
    reduce_scatter x1, waiting for transfers between devices, local(): lax.psum_scatter(term, 'sample', scatter_dimension=0, tiled=True) / 16.0  282 us
    all_gather x1, waiting for transfers between devices, local(): lax.all_gather(coef_low, 'sample', axis=0, tiled=True)  121 us
    scatter-add x1, other arithmetic, local(): jax.ops.segment_sum(back, cols, num_segments=col_blocks)  42.8 us
    scatter-add x1, other arithmetic, local(): jax.ops.segment_sum(products, rows, num_segments=row_blocks)  28.8 us
    psum x1, waiting for transfers between devices, local(): margins = lax.psum(partial_value, 'feature')  20 us
  transfers between devices with their start and end apart: 3, of which 3 were waited for; matrix products, arithmetic and copies ran while one was open for 0% of the time, Pallas kernels for 0%

commit v1 on v0

v1 whole, which is shorter than its diff:
```python
import functools

import jax
import jax.numpy as jnp
from jax import lax
from jax.experimental import pallas as pl
from jax.experimental.pallas import tpu as pltpu
from jax.sharding import PartitionSpec as P

MESH = pl.DeviceIdType.MESH
F32 = jnp.float32
BF16 = jnp.bfloat16


def _sizes(n, slots, row_blocks):
    quota = slots // n
    step = max(u for u in range(1, 11) if quota % u == 0)
    return quota, step


def _distance(n, i):
    half = (i + 1) // 2
    return n // 2 + (1 - 2 * (i % 2)) * half


def exchange_kernel(
    n,
    quota,
    step,
    row_blocks,
    meta,
    req_ref,
    coef_ref,
    counts_ref,
    labels_ref,
    values_ref,
    asked_ref,
    grad_ref,
    vbuf,
    blocks,
    send,
    recv,
    prod,
    run,
    marg,
    marg_other,
    resid,
    gsend,
    wanted,
    v_sem,
    req_send,
    req_recv,
    want_sem,
    c_send,
    c_recv,
    m_send,
    m_recv,
    g_send,
    g_recv,
    own_sem,
):
    me = lax.axis_index("sample")
    feat = lax.axis_index("feature")
    other = 1 - feat
    width = blocks.shape[2]
    slots = n * quota

    load_values = pltpu.make_async_copy(values_ref, vbuf, v_sem)
    load_values.start()

    barrier = pltpu.get_barrier_semaphore()
    for d in range(1, n):
        pl.semaphore_signal(
            barrier, inc=1, device_id={"sample": lax.rem(me + d, n)}, device_id_type=MESH
        )
    pl.semaphore_signal(barrier, inc=1, device_id={"feature": other}, device_id_type=MESH)
    pl.semaphore_wait(barrier, n)

    def req_copy(d):
        dst = lax.rem(me + d, n)
        return pltpu.make_async_remote_copy(
            src_ref=req_ref.at[dst],
            dst_ref=asked_ref.at[me],
            send_sem=req_send.at[d],
            recv_sem=req_recv.at[d],
            device_id={"sample": dst},
            device_id_type=MESH,
        )

    def coef_copy(d):
        dst = lax.rem(me + d, n)
        return pltpu.make_async_remote_copy(
            src_ref=send.at[dst],
            dst_ref=recv.at[me],
            send_sem=c_send.at[d],
            recv_sem=c_recv.at[d],
            device_id={"sample": dst},
            device_id_type=MESH,
        )

    def grad_copy(d):
        dst = lax.rem(me + d, n)
        return pltpu.make_async_remote_copy(
            src_ref=gsend.at[dst],
            dst_ref=grad_ref.at[me],
            send_sem=g_send.at[d],
            recv_sem=g_recv.at[d],
            device_id={"sample": dst},
            device_id_type=MESH,
        )

    for i in range(n - 1):
        req_copy(_distance(n, i)).start()

    asked_ref[me] = req_ref[me]
    for b in range(blocks.shape[0]):
        blocks[b] = coef_ref[:, b * width : (b + 1) * width].astype(BF16)

    def pack(source, target, src_slot, dst_slot):
        def some(g, carry):
            for u in range(step):
                j = g * step + u
                target[dst_slot, j] = blocks[wanted[src_slot, 0, j]]
            return carry

        lax.fori_loop(0, quota // step, some, 0)

    def serve(i, carry):
        d = n - _distance(n, i)
        dst = lax.rem(me + n - d, n)
        req_copy(d).wait_recv()
        bring = pltpu.make_async_copy(asked_ref.at[dst], wanted.at[dst], want_sem)
        bring.start()
        bring.wait()
        pack(wanted, send, dst, dst)
        coef_copy(n - d).start()
        return carry

    lax.fori_loop(0, n - 1, serve, 0)

    bring = pltpu.make_async_copy(asked_ref.at[me], wanted.at[me], want_sem)
    bring.start()
    bring.wait()
    pack(wanted, recv, me, me)
    load_values.wait()

    def forward(src):
        def some(g, carry):
            for u in range(step):
                j = g * step + u
                p = src * quota + j
                prod[p] = lax.dot_general(
                    recv[src, j],
                    vbuf[meta[0, p]],
                    (((1,), (1,)), ((), ())),
                    preferred_element_type=F32,
                )
            return carry

        lax.fori_loop(0, quota // step, some, 0)

    forward(me)

    def arrive(i, carry):
        d = _distance(n, i)
        coef_copy(d).wait_recv()
        forward(lax.rem(me + n - d, n))
        return carry

    lax.fori_loop(0, n - 1, arrive, 0)

    def rowsum(g, acc):
        for u in range(step):
            q = g * step + u
            acc = acc * meta[4, q].astype(F32) + prod[meta[3, q]]
            run[q] = acc
        return acc

    lax.fori_loop(0, slots // step, rowsum, jnp.zeros(marg.shape[1:], F32))

    def take(r, carry):
        marg[r] = run[meta[5, r]] * meta[6, r].astype(F32)
        return carry

    lax.fori_loop(0, row_blocks, take, 0)

    swap = pltpu.make_async_remote_copy(
        src_ref=marg,
        dst_ref=marg_other,
        send_sem=m_send,
        recv_sem=m_recv,
        device_id={"feature": other},
        device_id_type=MESH,
    )
    swap.start()
    swap.wait()

    def residual(r, carry):
        m = marg[r] + marg_other[r]
        at = pl.ds(pl.multiple_of(r * width, width), width)
        c = counts_ref[:, at].astype(F32)
        y = labels_ref[r].astype(F32)
        resid[r] = (c * (jax.nn.sigmoid(m) - y)).astype(BF16)
        return carry

    lax.fori_loop(0, row_blocks, residual, 0)

    def backward(dst):
        def some(g, carry):
            for u in range(step):
                j = g * step + u
                p = dst * quota + j
                back = lax.dot_general(
                    resid[meta[1, p]],
                    vbuf[meta[0, p]],
                    (((1,), (0,)), ((), ())),
                    preferred_element_type=F32,
                )
                gsend[dst, j] = (back * meta[2, p].astype(F32)).astype(BF16)
            return carry

        lax.fori_loop(0, quota // step, some, 0)

    def give(i, carry):
        d = _distance(n, i)
        backward(lax.rem(me + d, n))
        grad_copy(d).start()
        return carry

    lax.fori_loop(0, n - 1, give, 0)
    backward(me)
    keep = pltpu.make_async_copy(gsend.at[me], grad_ref.at[me], own_sem)
    keep.start()

    def finish(i, carry):
        d = _distance(n, i)
        req_copy(d).wait_send()
        coef_copy(d).wait_send()
        grad_copy(d).wait_send()
        grad_copy(d).wait_recv()
        return carry

    lax.fori_loop(0, n - 1, finish, 0)
    keep.wait()


def add_kernel(n, quota, step, scale, asked, grad_ref, out_ref):
    out_ref[...] = jnp.zeros_like(out_ref)
    width = grad_ref.shape[3]

    def source(s, carry):
        def some(g, inner):
            for u in range(step):
                j = g * step + u
                at = pl.ds(pl.multiple_of(asked[s, 0, j] * width, width), width)
                out_ref[:, at] += grad_ref[s, j].astype(F32) * scale
            return inner

        return lax.fori_loop(0, quota // step, some, carry)

    lax.fori_loop(0, n, source, 0)


def plan(rows, cols, count, n, quota, share, row_blocks):
    slots = rows.shape[0]
    ids = jnp.arange(slots, dtype=jnp.int32)
    owner = cols // share
    before = ids[None, :] < ids[:, None]
    same = (owner[:, None] == owner[None, :]) & before
    rank = owner * quota + jnp.sum(same.astype(jnp.int32), axis=1)
    live = (ids < count).astype(jnp.int32)
    key = jnp.where(ids < count, rows, row_blocks)
    ahead = (key[None, :] < key[:, None]) | ((key[None, :] == key[:, None]) & before)
    row_rank = jnp.sum(ahead.astype(jnp.int32), axis=1)
    code = ((cols % share) * 2 + live) * row_blocks + rows
    code = code * slots + ids
    by_owner = jnp.sum(jnp.where(rank[None, :] == ids[:, None], code[None, :], 0), axis=1)
    row_code = key * slots + rank
    by_row = jnp.sum(jnp.where(row_rank[None, :] == ids[:, None], row_code[None, :], 0), axis=1)
    order = by_owner % slots
    rest = by_owner // slots
    row_at = rest % row_blocks
    rest = rest // row_blocks
    live_at = rest % 2
    local_col = rest // 2
    row_order = by_row % slots
    key_at = by_row // slots
    keep = (key_at == jnp.roll(key_at, 1)).astype(jnp.int32)
    blocks = jnp.arange(slots, dtype=jnp.int32)
    upto = jnp.sum((key[None, :] <= blocks[:, None]).astype(jnp.int32), axis=1)
    here = jnp.sum((key[None, :] == blocks[:, None]).astype(jnp.int32), axis=1)
    last = jnp.maximum(upto - 1, 0)
    some = (here > 0).astype(jnp.int32)
    meta = jnp.stack([order, row_at, live_at, row_order, keep, last, some, keep])
    req = jnp.zeros((n, 8, 128), jnp.int32).at[:, :, :quota].set(
        local_col.reshape(n, 1, quota)
    )
    return meta, req


def local(blk_values, blk_rows, blk_cols, blk_count, boot_counts, labels, coefs):
    values = blk_values[0, 0]
    slots, width = values.shape[0], values.shape[1]
    reps = coefs.shape[1]
    n = lax.axis_size("sample")
    row_blocks = boot_counts.shape[0] // width
    share = coefs.shape[0] // width
    quota, step = _sizes(n, slots, row_blocks)
    meta, req = plan(
        blk_rows[0, 0], blk_cols[0, 0], blk_count[0, 0], n, quota, share, row_blocks
    )
    vmem = pl.BlockSpec(memory_space=pltpu.VMEM)
    smem = pl.BlockSpec(memory_space=pltpu.SMEM)
    hbm = pl.BlockSpec(memory_space=pl.ANY)
    asked, grads = pl.pallas_call(
        functools.partial(exchange_kernel, n, quota, step, row_blocks),
        out_shape=[
            jax.ShapeDtypeStruct((n, 8, 128), jnp.int32),
            jax.ShapeDtypeStruct((n, quota, reps, width), BF16),
        ],
        in_specs=[smem, vmem, vmem, vmem, vmem, hbm],
        out_specs=[vmem, hbm],
        scratch_shapes=[
            pltpu.VMEM((slots, width, width), BF16),
            pltpu.VMEM((share, reps, width), BF16),
            pltpu.VMEM((n, quota, reps, width), BF16),
            pltpu.VMEM((n, quota, reps, width), BF16),
            pltpu.VMEM((slots, reps, width), F32),
            pltpu.VMEM((slots, reps, width), F32),
            pltpu.VMEM((row_blocks, reps, width), F32),
            pltpu.VMEM((row_blocks, reps, width), F32),
            pltpu.VMEM((row_blocks, reps, width), BF16),
            pltpu.VMEM((n, quota, reps, width), BF16),
            pltpu.SMEM((n, 8, 128), jnp.int32),
            pltpu.SemaphoreType.DMA,
            pltpu.SemaphoreType.DMA((n,)),
            pltpu.SemaphoreType.DMA((n,)),
            pltpu.SemaphoreType.DMA,
            pltpu.SemaphoreType.DMA((n,)),
            pltpu.SemaphoreType.DMA((n,)),
            pltpu.SemaphoreType.DMA,
            pltpu.SemaphoreType.DMA,
            pltpu.SemaphoreType.DMA((n,)),
            pltpu.SemaphoreType.DMA((n,)),
            pltpu.SemaphoreType.DMA,
        ],
        compiler_params=pltpu.CompilerParams(
            collective_id=0, has_side_effects=True, vmem_limit_bytes=56 * 2**20
        ),
        name="exchange",
    )(meta, req, coefs.T, boot_counts.T, labels.reshape(row_blocks, 1, width), values)
    total = pl.pallas_call(
        functools.partial(add_kernel, n, quota, step, 1.0 / 16.0),
        out_shape=jax.ShapeDtypeStruct((reps, coefs.shape[0]), F32),
        in_specs=[smem, vmem],
        out_specs=vmem,
        compiler_params=pltpu.CompilerParams(vmem_limit_bytes=32 * 2**20),
        name="add",
    )(asked, grads)
    return total.T


def solution(mesh):
    return jax.shard_map(
        local,
        mesh=mesh,
        in_specs=(
            P(("groups", "sample"), "feature", None, None, None),
            P(("groups", "sample"), "feature", None),
            P(("groups", "sample"), "feature", None),
            P(("groups", "sample"), "feature"),
            P(("groups", "sample"), None),
            P(("groups", "sample")),
            P(("groups", "feature", "sample"), None),
        ),
        out_specs=P(("groups", "feature", "sample"), None),
        check_vma=False,
    )
```

time: 574 us -> 141 us (0.25)
  waiting for transfers between devices: 424 us -> 0 us
  Pallas kernels: 0 us -> 132 us
  other arithmetic: 80 us -> 3.04 us
  local copies, waits for them, and re-layouts: 35 us -> 4.49 us
  matrix products: 16.8 us -> 0 us
  between operations: 13.9 us -> 0.75 us
    reduce_scatter x1 -> x0, waiting for transfers between devices: 282 us -> none  [local(): lax.psum_scatter(term, 'sample', scatter_dimension=0, tiled=True) / 16.0]
    pallas_call x0 -> x2, Pallas kernels: none -> 132 us  [the longest x1 128 us: local(): pl.pallas_call(functools.partial(exchange_kernel, n, quota, step, row_blo...]
    all_gather x1 -> x0, waiting for transfers between devices: 121 us -> none  [local(): lax.all_gather(coef_low, 'sample', axis=0, tiled=True)]
    scatter-add x2 -> x0, other arithmetic: 71.6 us -> none  [the longest x1 42.8 us: local(): jax.ops.segment_sum(back, cols, num_segments=col_blocks)]
    reshape x3 -> x0, local copies, waits for them, and re-layouts: 20.2 us -> none  [the longest x1 11.3 us: local(): jax.ops.segment_sum(back, cols, num_segments=col_blocks)]
    psum x1 -> x0, waiting for transfers between devices: 20 us -> none  [local(): margins = lax.psum(partial_value, 'feature')]
    dot_general x2 -> x0, matrix products: 16.8 us -> none  [the longest x1 9.71 us: local(): jnp.einsum('bij,bjr->bir', values, whole[cols], preferred_element_type=jn...]
    broadcast_in_dim x2 -> x0, local copies, waits for them, and re-layouts: 7.91 us -> none  [the longest x1 7.86 us: local(): jax.ops.segment_sum(back, cols, num_segments=col_blocks)]
  transfers between devices with their start and end apart: 3 -> 0, of which waited for: 3 -> 0; matrix products, arithmetic and copies ran while one was open for 0% -> 0% of each run, Pallas kernels for 0% -> 0%
where the time goes in v1:
time: 141 us; the launch traced here: 140 us
  Pallas kernels  132 us (94%)
  local copies, waits for them, and re-layouts  4.49 us (3%)
  other arithmetic  3.04 us (2%)
    pallas_call x1, Pallas kernels, local(): pl.pallas_call(functools.partial(exchange_kernel, n, quota, step, row_blo...  128 us
    pallas_call x1, Pallas kernels, local(): pl.pallas_call(functools.partial(add_kernel, n, quota, step, 1.0 / 16.0),...  4.41 us

profile of v1, /device:TPU:14, one launch (start us, length us, event | category | flops | bytes accessed | tf_op | source)
XLA Modules:
  0.0 140.4 jit_solution(9784051402406860278)
XLA Ops:
  0.7 0.7 reduce.2
  1.4 0.2 convert_reduce_fusion.3
  1.6 0.7 reduce.3
  2.3 0.4 convert_reduce_fusion
  2.7 0.2 select_reduce_fusion
  2.9 0.1 and.194
  3.1 0.1 div.89
  3.2 0.6 slice.29
  3.8 0.7 compare_convert_fusion
  4.5 0.6 stack.2.meta
  5.1 0.6 scatter.4.req_ref
  5.8 127.7 %exchange.1 = (s32[8,8,128]{2,1,0:T(8,128)}, bf16[8,40,32,128]{3,2,1,0:T(8,128)(2,1)}) custom-call(s32[8,320]{1,0:T(8,128)} %stack.2.meta, s32[8,8,128]{2,1,0:T(8,128)} %scatter.4.req_ref, f32[32,16384]{1,0:T(8,128)} %bitcast.10, s32[32,4096]{1,0:T(8,128)} %bitcast.11, s32[32,1,128]{2,1,0:T(1,128)} %bitcast.12, bf16[320,128,128]{2,1,0:T(8,128)(2,1)} %bitcast.9), custom_call_target="tpu_custom_call" | custom-call | tf_op jit(solution)/shard_map/exchange/pallas_call | solution.py:315
  133.5 0.0 copy-start
  133.5 1.7 %copy-done = bf16[8,40,32,128]{3,2,1,0:T(8,128)(2,1)S(1)} copy-done((bf16[8,40,32,128]{3,2,1,0:T(8,128)(2,1)S(1)}, bf16[8,40,32,128]{3,2,1,0:T(8,128)(2,1)}, u32[]{:S(2)}) %copy-start) | copy-done | bytes 2621464
  135.2 0.0 copy-start.1
  135.2 0.8 copy-done.1
  136.0 4.4 %add.211 = f32[32,16384]{1,0:T(8,128)} custom-call(s32[8,8,128]{2,1,0:T(8,128)S(1)} %copy-done.1, bf16[8,40,32,128]{3,2,1,0:T(8,128)(2,1)S(1)} %copy-done), custom_call_target="tpu_custom_call" | custom-call | tf_op jit(solution)/shard_map/add/pallas_call | solution.py:352
  (16 shorter events, 0.2 us)
Async XLA Ops:
  133.5 1.7 %copy-start = (bf16[8,40,32,128]{3,2,1,0:T(8,128)(2,1)S(1)}, bf16[8,40,32,128]{3,2,1,0:T(8,128)(2,1)}, u32[]{:S(2)}) copy-start(bf16[8,40,32,128]{3,2,1,0:T(8,128)(2,1)} %get-tuple-element.20.grad_ref) | copy-start | bytes 7864324
  135.2 0.8 copy-start.1

commit v2 on v1

v2 whole, which is shorter than its diff:
```python
import functools

import jax
import jax.numpy as jnp
from jax import lax
from jax.experimental import pallas as pl
from jax.experimental.pallas import tpu as pltpu
from jax.sharding import PartitionSpec as P

MESH = pl.DeviceIdType.MESH
F32 = jnp.float32
BF16 = jnp.bfloat16


PARTS = 2


def _sizes(n, slots):
    quota = slots // n
    step = max(u for u in range(1, 11) if quota % u == 0)
    return quota, step


def _distance(n, i):
    half = (i + 1) // 2
    return n // 2 + (1 - 2 * (i % 2)) * half


def _bits(size):
    return (size - 1).bit_length()


def exchange_kernel(
    n,
    quota,
    step,
    row_blocks,
    count_ref,
    rows_ref,
    cols_ref,
    coef_ref,
    counts_ref,
    labels_ref,
    values_ref,
    asked_out,
    grad_ref,
    vbuf,
    blocks,
    send,
    recv,
    prod,
    run,
    marg,
    marg_other,
    resid,
    gsend,
    plan,
    asked,
    sums,
    wanted,
    mine,
    meta,
    v_sem,
    req_send,
    req_recv,
    want_sem,
    asked_sem,
    c_send,
    c_recv,
    m_send,
    m_recv,
    g_send,
    g_recv,
    own_sem,
):
    me = lax.axis_index("sample")
    feat = lax.axis_index("feature")
    other = 1 - feat
    share, reps, width = blocks.shape[1:]
    slots = n * quota
    i32 = jnp.int32

    load_values = pltpu.make_async_copy(values_ref, vbuf, v_sem)
    load_values.start()

    barrier = pltpu.get_barrier_semaphore()
    for d in range(1, n):
        pl.semaphore_signal(
            barrier, inc=1, device_id={"sample": lax.rem(me + d, n)}, device_id_type=MESH
        )
    pl.semaphore_signal(barrier, inc=1, device_id={"feature": other}, device_id_type=MESH)

    ii = lax.broadcasted_iota(i32, (slots, slots), 0)
    jj = lax.broadcasted_iota(i32, (slots, slots), 1)

    def upright(row):
        return jnp.sum(jnp.where(ii == jj, row, 0), axis=1, keepdims=True)

    share_bits, row_bits, slot_bits = _bits(share), _bits(row_blocks), _bits(slots)
    cols = cols_ref[...]
    rows = rows_ref[...]
    ids = lax.broadcasted_iota(i32, (1, slots), 1)
    live = (ids < count_ref[0, 0]).astype(i32)
    owner = lax.shift_right_logical(cols, jnp.full_like(cols, share_bits))
    owner_up = upright(owner)
    same = jnp.where((owner_up == owner) & (jj < ii), 1, 0)
    rank = owner_up * quota + jnp.sum(same, axis=1, keepdims=True)
    code = (cols & (share - 1)) * 2 + live
    code = (code * (1 << row_bits) + rows) * (1 << slot_bits) + ids
    code_up = upright(code)
    lane = lax.broadcasted_iota(i32, (slots, 128), 1)

    def shifted(x, bits):
        return lax.shift_right_logical(x, jnp.full_like(x, bits))

    for k in range(n):
        hit = (rank == lane + k * quota) & (lane < quota)
        found = jnp.sum(jnp.where(hit, code_up, 0), axis=0, keepdims=True)
        plan[k, 0:1, :] = shifted(found, slot_bits + row_bits + 1)
        plan[k, 1:2, :] = found & ((1 << slot_bits) - 1)
        plan[k, 2:3, :] = shifted(found, slot_bits) & ((1 << row_bits) - 1)
        plan[k, 3:4, :] = shifted(found, slot_bits + row_bits) & 1
        plan[k, 4:8, :] = jnp.zeros((4, 128), i32)

    pl.semaphore_wait(barrier, n)

    def req_copy(d):
        dst = lax.rem(me + d, n)
        return pltpu.make_async_remote_copy(
            src_ref=plan.at[dst],
            dst_ref=asked.at[me],
            send_sem=req_send.at[d],
            recv_sem=req_recv.at[d],
            device_id={"sample": dst},
            device_id_type=MESH,
        )

    def coef_copy(h, d):
        dst = lax.rem(me + d, n)
        return pltpu.make_async_remote_copy(
            src_ref=send.at[h, dst],
            dst_ref=recv.at[h, me],
            send_sem=c_send.at[h, d],
            recv_sem=c_recv.at[h, d],
            device_id={"sample": dst},
            device_id_type=MESH,
        )

    def grad_copy(h, d):
        dst = lax.rem(me + d, n)
        return pltpu.make_async_remote_copy(
            src_ref=gsend.at[h, dst],
            dst_ref=grad_ref.at[h, me],
            send_sem=g_send.at[h, d],
            recv_sem=g_recv.at[h, d],
            device_id={"sample": dst},
            device_id_type=MESH,
        )

    def swap_copy(h):
        return pltpu.make_async_remote_copy(
            src_ref=marg.at[h],
            dst_ref=marg_other.at[h],
            send_sem=m_send.at[h],
            recv_sem=m_recv.at[h],
            device_id={"feature": other},
            device_id_type=MESH,
        )

    for i in range(n - 1):
        req_copy(_distance(n, i)).start()

    bring_mine = pltpu.make_async_copy(plan, mine, want_sem.at[0])
    bring_mine.start()
    for h in range(PARTS):
        for b in range(share):
            at = slice(b * width, (b + 1) * width)
            blocks[h, b] = coef_ref[h * reps : (h + 1) * reps, at].astype(BF16)
    asked[me] = plan[me]
    bring_mine.wait()

    def pack(h, table, target, slot):
        def some(g, carry):
            for u in range(step):
                j = g * step + u
                target[h, slot, j] = blocks[h, table[slot, 0, j]]
            return carry

        lax.fori_loop(0, quota // step, some, 0)

    def serve(i, carry):
        up = _distance(n, i)
        src = lax.rem(me + up, n)
        req_copy(n - up).wait_recv()
        bring = pltpu.make_async_copy(asked.at[src], wanted.at[src], want_sem.at[1])
        bring.start()
        bring.wait()
        pack(0, wanted, send, src)
        coef_copy(0, up).start()
        return carry

    lax.fori_loop(0, n - 1, serve, 0)
    keep_asked = pltpu.make_async_copy(asked, asked_out, asked_sem)
    keep_asked.start()

    def prepare(i, carry):
        pack(1, wanted, send, lax.rem(me + i, n))
        return carry

    lax.fori_loop(1, n, prepare, 0)
    for h in range(PARTS):
        pack(h, mine, recv, me)

    key = jnp.where(live > 0, rows, row_blocks)
    key_up = upright(key)
    ahead = jnp.where((key < key_up) | ((key == key_up) & (jj < ii)), 1, 0)
    row_rank = jnp.sum(ahead, axis=1, keepdims=True)

    def by_row(shift, column):
        return jnp.sum(jnp.where(row_rank + shift == jj, column, 0), axis=0, keepdims=True)

    sums[...] = jnp.zeros_like(sums)
    sums[0:1, 0:slots] = by_row(0, rank)
    sums[1:2, 0:slots] = jnp.where(by_row(0, key_up) == by_row(1, key_up), 1, 0)
    upto = jnp.sum(jnp.where(key_up <= lane, 1, 0), axis=0, keepdims=True)
    here = jnp.sum(jnp.where(key_up == lane, 1, 0), axis=0, keepdims=True)
    sums[2:3, 0:128] = jnp.maximum(upto - 1, 0)
    sums[3:4, 0:128] = jnp.minimum(here, 1)
    bring_sums = pltpu.make_async_copy(sums, meta, want_sem.at[0])
    bring_sums.start()
    bring_sums.wait()
    load_values.wait()

    def forward(h, src):
        def some(g, carry):
            for u in range(step):
                j = g * step + u
                prod[src * quota + j] = lax.dot_general(
                    recv[h, src, j],
                    vbuf[mine[src, 1, j]],
                    (((1,), (1,)), ((), ())),
                    preferred_element_type=F32,
                )
            return carry

        lax.fori_loop(0, quota // step, some, 0)

    def row_sums(h):
        def one(g, acc):
            for u in range(step):
                q = g * step + u
                acc = acc * meta[1, q].astype(F32) + prod[meta[0, q]]
                run[q] = acc
            return acc

        lax.fori_loop(0, slots // step, one, jnp.zeros((reps, width), F32))

        def take(r, carry):
            marg[h, r] = run[meta[2, r]] * meta[3, r].astype(F32)
            return carry

        lax.fori_loop(0, row_blocks, take, 0)

    def residuals(h):
        def one(r, carry):
            m = marg[h, r] + marg_other[h, r]
            at = pl.ds(pl.multiple_of(r * width, width), width)
            c = counts_ref[h * reps : (h + 1) * reps, at].astype(F32)
            y = labels_ref[r].astype(F32)
            resid[h, r] = (c * (jax.nn.sigmoid(m) - y)).astype(BF16)
            return carry

        lax.fori_loop(0, row_blocks, one, 0)

    def backward(h, dst):
        def some(g, carry):
            for u in range(step):
                j = g * step + u
                back = lax.dot_general(
                    resid[h, mine[dst, 2, j]],
                    vbuf[mine[dst, 1, j]],
                    (((1,), (0,)), ((), ())),
                    preferred_element_type=F32,
                )
                gsend[h, dst, j] = (back * mine[dst, 3, j].astype(F32)).astype(BF16)
            return carry

        lax.fori_loop(0, quota // step, some, 0)

    def own_copy(h):
        return pltpu.make_async_copy(gsend.at[h, me], grad_ref.at[h, me], own_sem.at[h])

    forward(0, me)

    def arrive_first(i, carry):
        d = _distance(n, i)
        coef_copy(0, d).wait_send()
        coef_copy(1, d).start()
        coef_copy(0, d).wait_recv()
        forward(0, lax.rem(me + n - d, n))
        return carry

    lax.fori_loop(0, n - 1, arrive_first, 0)
    row_sums(0)
    swap_copy(0).start()
    forward(1, me)
    swap_copy(0).wait()
    residuals(0)

    def give_first(i, carry):
        d = _distance(n, i)
        backward(0, lax.rem(me + d, n))
        coef_copy(1, d).wait_send()
        grad_copy(0, d).start()
        return carry

    lax.fori_loop(0, n - 1, give_first, 0)
    backward(0, me)
    own_copy(0).start()

    def arrive_second(i, carry):
        d = _distance(n, i)
        coef_copy(1, d).wait_recv()
        forward(1, lax.rem(me + n - d, n))
        return carry

    lax.fori_loop(0, n - 1, arrive_second, 0)
    row_sums(1)
    swap_copy(1).start()
    swap_copy(1).wait()
    residuals(1)

    def give_second(i, carry):
        d = _distance(n, i)
        backward(1, lax.rem(me + d, n))
        grad_copy(1, d).start()
        return carry

    lax.fori_loop(0, n - 1, give_second, 0)
    backward(1, me)
    own_copy(1).start()

    def finish(i, carry):
        d = _distance(n, i)
        req_copy(d).wait_send()
        for h in range(PARTS):
            grad_copy(h, d).wait_send()
            grad_copy(h, d).wait_recv()
        return carry

    lax.fori_loop(0, n - 1, finish, 0)
    keep_asked.wait()
    for h in range(PARTS):
        own_copy(h).wait()


def add_kernel(n, quota, step, scale, asked_ref, grad_ref, out_ref, gbuf, asked, sems, asked_sem):
    reps, width = gbuf.shape[3:]

    def fetch(h, s):
        return pltpu.make_async_copy(grad_ref.at[h, s], gbuf.at[h, s], sems.at[h, s])

    bring = pltpu.make_async_copy(asked_ref, asked, asked_sem)
    bring.start()
    for s in range(n):
        for h in range(PARTS):
            fetch(h, s).start()
    out_ref[...] = jnp.zeros_like(out_ref)
    bring.wait()

    def source(s, carry):
        for h in range(PARTS):
            fetch(h, s).wait()

        def some(g, inner):
            for u in range(step):
                j = g * step + u
                at = pl.ds(pl.multiple_of(asked[s, 0, j] * width, width), width)
                for h in range(PARTS):
                    out_ref[h * reps : (h + 1) * reps, at] += gbuf[h, s, j].astype(F32) * scale
            return inner

        return lax.fori_loop(0, quota // step, some, carry)

    lax.fori_loop(0, n, source, 0)


def local(blk_values, blk_rows, blk_cols, blk_count, boot_counts, labels, coefs):
    values = blk_values[0, 0]
    slots, width = values.shape[0], values.shape[1]
    reps = coefs.shape[1] // PARTS
    n = lax.axis_size("sample")
    row_blocks = boot_counts.shape[0] // width
    share = coefs.shape[0] // width
    quota, step = _sizes(n, slots)
    wide = -(-slots // 128) * 128
    vmem = pl.BlockSpec(memory_space=pltpu.VMEM)
    smem = pl.BlockSpec(memory_space=pltpu.SMEM)
    hbm = pl.BlockSpec(memory_space=pl.ANY)
    dma = pltpu.SemaphoreType.DMA
    per_owner = (PARTS, n, quota, reps, width)
    per_row = (PARTS, row_blocks, reps, width)
    asked, grads = pl.pallas_call(
        functools.partial(exchange_kernel, n, quota, step, row_blocks),
        out_shape=[
            jax.ShapeDtypeStruct((n, 8, 128), jnp.int32),
            jax.ShapeDtypeStruct(per_owner, BF16),
        ],
        in_specs=[smem, vmem, vmem, vmem, vmem, vmem, hbm],
        out_specs=[hbm, hbm],
        scratch_shapes=[
            pltpu.VMEM((slots, width, width), BF16),
            pltpu.VMEM((PARTS, share, reps, width), BF16),
            pltpu.VMEM(per_owner, BF16),
            pltpu.VMEM(per_owner, BF16),
            pltpu.VMEM((slots, reps, width), F32),
            pltpu.VMEM((slots, reps, width), F32),
            pltpu.VMEM(per_row, F32),
            pltpu.VMEM(per_row, F32),
            pltpu.VMEM(per_row, BF16),
            pltpu.VMEM(per_owner, BF16),
            pltpu.VMEM((n, 8, 128), jnp.int32),
            pltpu.VMEM((n, 8, 128), jnp.int32),
            pltpu.VMEM((8, wide), jnp.int32),
            pltpu.SMEM((n, 8, 128), jnp.int32),
            pltpu.SMEM((n, 8, 128), jnp.int32),
            pltpu.SMEM((8, wide), jnp.int32),
            dma,
            dma((n,)),
            dma((n,)),
            dma((2,)),
            dma,
            dma((PARTS, n)),
            dma((PARTS, n)),
            dma((PARTS,)),
            dma((PARTS,)),
            dma((PARTS, n)),
            dma((PARTS, n)),
            dma((PARTS,)),
        ],
        compiler_params=pltpu.CompilerParams(
            collective_id=0, has_side_effects=True, vmem_limit_bytes=56 * 2**20
        ),
        name="exchange",
    )(
        blk_count,
        blk_rows[0],
        blk_cols[0],
        coefs.T,
        boot_counts.T,
        labels.reshape(row_blocks, 1, width),
        values,
    )
    total = pl.pallas_call(
        functools.partial(add_kernel, n, quota, step, 1.0 / 16.0),
        out_shape=jax.ShapeDtypeStruct((PARTS * reps, coefs.shape[0]), F32),
        in_specs=[hbm, hbm],
        out_specs=vmem,
        scratch_shapes=[
            pltpu.VMEM(per_owner, BF16),
            pltpu.SMEM((n, 8, 128), jnp.int32),
            dma((PARTS, n)),
            dma,
        ],
        compiler_params=pltpu.CompilerParams(vmem_limit_bytes=56 * 2**20),
        name="add",
    )(asked, grads)
    return total.T


def solution(mesh):
    return jax.shard_map(
        local,
        mesh=mesh,
        in_specs=(
            P(("groups", "sample"), "feature", None, None, None),
            P(("groups", "sample"), "feature", None),
            P(("groups", "sample"), "feature", None),
            P(("groups", "sample"), "feature"),
            P(("groups", "sample"), None),
            P(("groups", "sample")),
            P(("groups", "feature", "sample"), None),
        ),
        out_specs=P(("groups", "feature", "sample"), None),
        check_vma=False,
    )
```

time: 141 us -> 129 us (0.915)
  local copies, waits for them, and re-layouts: 4.49 us -> 0 us
  Pallas kernels: 132 us -> 128 us
  other arithmetic: 3.04 us -> 0 us
    pallas_call x1, Pallas kernels: 128 us -> 124 us  [local(): pl.pallas_call(functools.partial(exchange_kernel, n, quota, step, row_blo...]
    unnamed x4 -> x0, local copies, waits for them, and re-layouts: 2.49 us -> none
where the time goes in v2:
time: 129 us
  Pallas kernels  128 us (99%)
    pallas_call x1, Pallas kernels, local(): pl.pallas_call(functools.partial(exchange_kernel, n, quota, step, row_blo...  124 us
    pallas_call x1, Pallas kernels, local(): pl.pallas_call(functools.partial(add_kernel, n, quota, step, 1.0 / 16.0),...  4.7 us

profile of v2, /device:TPU:14, one launch (start us, length us, event | category | flops | bytes accessed | tf_op | source)
XLA Modules:
  0.0 128.9 jit_solution(14632028458161472932)
XLA Ops:
  0.7 123.6 %exchange.1 = (s32[8,8,128]{2,1,0:T(8,128)}, bf16[2,8,40,16,128]{4,3,2,1,0:T(8,128)(2,1)}) custom-call(s32[1,1]{1,0:T(1,128)S(6)} %copy.8.count_ref, s32[1,320]{1,0:T(1,128)} %bitcast.11, s32[1,320]{1,0:T(1,128)} %bitcast.12, f32[32,16384]{1,0:T(8,128)} %bitcast.8, s32[32,4096]{1,0:T(8,128)} %bitcast.9, s32[32,1,128]{2,1,0:T(1,128)} %bitcast.10, ...), custom_call_target="tpu_custom_call" | custom-call | tf_op jit(solution)/shard_map/exchange/pallas_call | solution.py:403
  124.2 4.7 %add.1 = f32[32,16384]{1,0:T(8,128)} custom-call(s32[8,8,128]{2,1,0:T(8,128)} %get-tuple-element.7.asked_ref, bf16[2,8,40,16,128]{4,3,2,1,0:T(8,128)(2,1)} %get-tuple-element.8.grad_ref), custom_call_target="tpu_custom_call" | custom-call | tf_op jit(solution)/shard_map/add/pallas_call | solution.py:454

commit v3 on v2

--- a/solution.py
+++ b/solution.py
@@ -38,12 +38,14 @@
     count_ref,
     rows_ref,
     cols_ref,
-    coef_ref,
-    counts_ref,
     labels_ref,
+    coef_hbm,
+    counts_hbm,
     values_ref,
     asked_out,
     grad_ref,
+    coef_ref,
+    counts_ref,
     vbuf,
     blocks,
     send,
@@ -80,8 +82,10 @@
     slots = n * quota
     i32 = jnp.int32
 
-    load_values = pltpu.make_async_copy(values_ref, vbuf, v_sem)
-    load_values.start()
+    load_coefs = pltpu.make_async_copy(coef_hbm, coef_ref, v_sem.at[0])
+    load_coefs.start()
+    load_counts = pltpu.make_async_copy(counts_hbm, counts_ref, v_sem.at[1])
+    load_values = pltpu.make_async_copy(values_ref, vbuf, v_sem.at[2])
 
     barrier = pltpu.get_barrier_semaphore()
     for d in range(1, n):
@@ -172,12 +176,17 @@
 
     bring_mine = pltpu.make_async_copy(plan, mine, want_sem.at[0])
     bring_mine.start()
-    for h in range(PARTS):
+
+    def round_blocks(h):
         for b in range(share):
             at = slice(b * width, (b + 1) * width)
             blocks[h, b] = coef_ref[h * reps : (h + 1) * reps, at].astype(BF16)
+
     asked[me] = plan[me]
-    bring_mine.wait()
+    load_coefs.wait()
+    load_values.start()
+    load_counts.start()
+    round_blocks(0)
 
     def pack(h, table, target, slot):
         def some(g, carry):
@@ -188,18 +197,24 @@
 
         lax.fori_loop(0, quota // step, some, 0)
 
+    def hear(i, carry):
+        req_copy(i).wait_recv()
+        return carry
+
+    lax.fori_loop(1, n, hear, 0)
+    bring = pltpu.make_async_copy(asked, wanted, want_sem.at[1])
+    bring.start()
+    bring.wait()
+
     def serve(i, carry):
         up = _distance(n, i)
-        src = lax.rem(me + up, n)
-        req_copy(n - up).wait_recv()
-        bring = pltpu.make_async_copy(asked.at[src], wanted.at[src], want_sem.at[1])
-        bring.start()
-        bring.wait()
-        pack(0, wanted, send, src)
+        pack(0, wanted, send, lax.rem(me + up, n))
         coef_copy(0, up).start()
         return carry
 
     lax.fori_loop(0, n - 1, serve, 0)
+    round_blocks(1)
+    bring_mine.wait()
     keep_asked = pltpu.make_async_copy(asked, asked_out, asked_sem)
     keep_asked.start()
 
@@ -230,6 +245,7 @@
     bring_sums.start()
     bring_sums.wait()
     load_values.wait()
+    load_counts.wait()
 
     def forward(h, src):
         def some(g, carry):
@@ -354,7 +370,7 @@
         own_copy(h).wait()
 
 
-def add_kernel(n, quota, step, scale, asked_ref, grad_ref, out_ref, gbuf, asked, sems, asked_sem):
+def add_kernel(n, quota, step, scale, asked_ref, grad_ref, out_ref, low, high, gbuf, asked, sems, asked_sem, out_sem):
     reps, width = gbuf.shape[3:]
 
     def fetch(h, s):
@@ -365,7 +381,9 @@
     for s in range(n):
         for h in range(PARTS):
             fetch(h, s).start()
-    out_ref[...] = jnp.zeros_like(out_ref)
+    totals = (low, high)
+    for total in totals:
+        total[...] = jnp.zeros_like(total)
     bring.wait()
 
     def source(s, carry):
@@ -377,12 +395,22 @@
                 j = g * step + u
                 at = pl.ds(pl.multiple_of(asked[s, 0, j] * width, width), width)
                 for h in range(PARTS):
-                    out_ref[h * reps : (h + 1) * reps, at] += gbuf[h, s, j].astype(F32) * scale
+                    totals[h][:, at] += gbuf[h, s, j].astype(F32) * scale
             return inner
 
         return lax.fori_loop(0, quota // step, some, carry)
 
     lax.fori_loop(0, n, source, 0)
+    stores = [
+        pltpu.make_async_copy(
+            totals[h], out_ref.at[pl.ds(h * reps, reps)], out_sem.at[h]
+        )
+        for h in range(PARTS)
+    ]
+    for store in stores:
+        store.start()
+    for store in stores:
+        store.wait()
 
 
 def local(blk_values, blk_rows, blk_cols, blk_count, boot_counts, labels, coefs):
@@ -406,9 +434,11 @@
             jax.ShapeDtypeStruct((n, 8, 128), jnp.int32),
             jax.ShapeDtypeStruct(per_owner, BF16),
         ],
-        in_specs=[smem, vmem, vmem, vmem, vmem, vmem, hbm],
+        in_specs=[smem, vmem, vmem, vmem, hbm, hbm, hbm],
         out_specs=[hbm, hbm],
         scratch_shapes=[
+            pltpu.VMEM((PARTS * reps, coefs.shape[0]), F32),
+            pltpu.VMEM((PARTS * reps, boot_counts.shape[0]), jnp.int32),
             pltpu.VMEM((slots, width, width), BF16),
             pltpu.VMEM((PARTS, share, reps, width), BF16),
             pltpu.VMEM(per_owner, BF16),
@@ -425,7 +455,7 @@
             pltpu.SMEM((n, 8, 128), jnp.int32),
             pltpu.SMEM((n, 8, 128), jnp.int32),
             pltpu.SMEM((8, wide), jnp.int32),
-            dma,
+            dma((3,)),
             dma((n,)),
             dma((n,)),
             dma((2,)),
@@ -446,21 +476,24 @@
         blk_count,
         blk_rows[0],
         blk_cols[0],
+        labels.reshape(row_blocks, 1, width),
         coefs.T,
         boot_counts.T,
-        labels.reshape(row_blocks, 1, width),
         values,
     )
     total = pl.pallas_call(
         functools.partial(add_kernel, n, quota, step, 1.0 / 16.0),
         out_shape=jax.ShapeDtypeStruct((PARTS * reps, coefs.shape[0]), F32),
         in_specs=[hbm, hbm],
-        out_specs=vmem,
+        out_specs=hbm,
         scratch_shapes=[
+            pltpu.VMEM((reps, coefs.shape[0]), F32),
+            pltpu.VMEM((reps, coefs.shape[0]), F32),
             pltpu.VMEM(per_owner, BF16),
             pltpu.SMEM((n, 8, 128), jnp.int32),
             dma((PARTS, n)),
             dma,
+            dma((PARTS,)),
         ],
         compiler_params=pltpu.CompilerParams(vmem_limit_bytes=56 * 2**20),
         name="add",

time: 129 us -> 129 us (level)
  no operation moved by 1% of the time
where the time goes in v3:
time: 129 us; the launch traced here: 128 us
  Pallas kernels  128 us (99%)
    pallas_call x1, Pallas kernels, local(): pl.pallas_call(functools.partial(exchange_kernel, n, quota, step, row_blo...  123 us
    pallas_call x1, Pallas kernels, local(): pl.pallas_call(functools.partial(add_kernel, n, quota, step, 1.0 / 16.0),...  4.64 us

profile of v3, /device:TPU:14, one launch (start us, length us, event | category | flops | bytes accessed | tf_op | source)
XLA Modules:
  0.0 128.3 jit_solution(3991171096862170363)
XLA Ops:
  0.7 123.0 %exchange.1 = (s32[8,8,128]{2,1,0:T(8,128)}, bf16[2,8,40,16,128]{4,3,2,1,0:T(8,128)(2,1)}) custom-call(s32[1,1]{1,0:T(1,128)S(6)} %copy.8.count_ref, s32[1,320]{1,0:T(1,128)} %bitcast.11, s32[1,320]{1,0:T(1,128)} %bitcast.12, s32[32,1,128]{2,1,0:T(1,128)} %bitcast.10, f32[32,16384]{1,0:T(8,128)} %bitcast.8, s32[32,4096]{1,0:T(8,128)} %bitcast.9, ...), custom_call_target="tpu_custom_call" | custom-call | tf_op jit(solution)/shard_map/exchange/pallas_call | solution.py:431
  123.7 4.6 %add.1 = f32[32,16384]{1,0:T(8,128)} custom-call(s32[8,8,128]{2,1,0:T(8,128)} %get-tuple-element.7.asked_ref, bf16[2,8,40,16,128]{4,3,2,1,0:T(8,128)(2,1)} %get-tuple-element.8.grad_ref), custom_call_target="tpu_custom_call" | custom-call | tf_op jit(solution)/shard_map/add/pallas_call | solution.py:484
